TPU v7x, 256 devices: a whole 4x4x8 slice. The times are simulated.
256 devices in a mesh: seq: 64 (over y, z, core), chan: 4 (over x).
Axes of the slice: x: 4, y: 4, z: 8, core: 2. Of those that a mesh axis runs over, the one named last changes fastest.
Arguments:
- inputs: bfloat16 [32768, 1536], P('seq', 'chan'), may hold values from -16 to 16
- conv_weight: bfloat16 [1, 3, 1536, 1536], P(None, None, None, 'chan'), may hold values from -0.09375 to 0.09375
- head_weight: bfloat16 [1536, 4096], P(None, 'chan'), may hold values from -0.15625 to 0.15625
- head_cot: bfloat16 [32768, 4096], P('seq', 'chan'), may hold values from -6 to 6
- exon_blocks: int32 [512, 8], P('seq'), may hold values from 0 to 255
Outputs:
- tracks: bfloat16 [32768, 4096], P('seq', 'chan')
- coverage: float32 [512, 4096], P('seq', 'chan')
- input_grad: bfloat16 [32768, 1536], P('seq', 'chan')
- kernel_gradient: float32 [1, 3, 1536, 1536], P(None, None, 'seq', 'chan')
All inputs are finite; a program needn't handle non-finite values.
Results may differ from a plain program's by a relative error of at most 0.0059.
Values may be sent and summed in bfloat16 or wider, within the bound.
No kernel may reach another device: no remote copies, remote signals or barrier semaphores. Data moves between devices by JAX's collectives and lax.ppermute only.
A program may use at most 64 MiB of HBM per device.

v0:
```python
import jax
import jax.numpy as jnp
from jax import lax
from jax.sharding import PartitionSpec as P

BLOCK = 128
EXONS = 8


def shifted(value, axis, steps):
    count = lax.axis_size(axis)
    leading, last = (max(0, -steps), min(count, count - steps))
    return lax.ppermute(value, axis, [(source, source + steps) for source in range(leading, last)])


def activation_slope(point, cotan):
    _, back = jax.vjp(jax.nn.gelu, point)
    return back(cotan)[0]


def tap_input(values, steps):
    return shifted(values, "seq", steps)


def tap_grad(values, steps):
    return shifted(values, "seq", steps)


def times_t(left, right):
    return lax.dot_general(
        left, right, (((1,), (1,)), ((), ())), preferred_element_type=jnp.float32
    )


def inner_rows(left, right):
    return lax.dot_general(
        left, right, (((0,), (0,)), ((), ())), preferred_element_type=jnp.float32
    )


def shards(inputs, conv_weight, head_weight, head_cot, exon_blocks):
    rows = inputs.shape[0]
    state = inputs
    layer_number = 0
    steps = 2 * 2**layer_number
    acted = jax.nn.gelu(state.astype(jnp.float32)).astype(jnp.bfloat16)
    lower = tap_input(acted, steps)
    upper = tap_input(acted, -steps)
    whole = lax.all_gather(acted, "chan", axis=1, tiled=True)
    whole_low = lax.all_gather(lower, "chan", axis=1, tiled=True)
    whole_up = lax.all_gather(upper, "chan", axis=1, tiled=True)
    mixed = jnp.dot(whole_low, conv_weight[layer_number, 0], preferred_element_type=jnp.float32)
    mixed = mixed + jnp.dot(whole, conv_weight[layer_number, 1], preferred_element_type=jnp.float32)
    mixed = mixed + jnp.dot(
        whole_up, conv_weight[layer_number, 2], preferred_element_type=jnp.float32
    )
    saved = [(state, whole, steps)]
    state = (state.astype(jnp.float32) + mixed).astype(jnp.bfloat16)
    full_state = lax.all_gather(state, "chan", axis=1, tiled=True)
    logits = jnp.dot(full_state, head_weight, preferred_element_type=jnp.float32)
    tracks = jax.nn.softplus(logits).astype(jnp.bfloat16)
    head_term = (head_cot.astype(jnp.float32) * jax.nn.sigmoid(logits)).astype(jnp.bfloat16)
    grad = lax.psum_scatter(
        times_t(head_term, head_weight), "chan", scatter_dimension=1, tiled=True
    )
    grads = []
    for layer_number in reversed(range(conv_weight.shape[0])):
        before, whole, steps = saved[layer_number]
        grad_low = grad.astype(jnp.bfloat16)
        later = tap_grad(grad_low, -steps)
        earlier = tap_grad(grad_low, steps)
        partial_value = times_t(later, conv_weight[layer_number, 0])
        partial_value = partial_value + times_t(grad_low, conv_weight[layer_number, 1])
        partial_value = partial_value + times_t(earlier, conv_weight[layer_number, 2])
        back_u = lax.psum_scatter(partial_value, "chan", scatter_dimension=1, tiled=True)
        kernel = jnp.stack(
            [inner_rows(whole, later), inner_rows(whole, grad_low), inner_rows(whole, earlier)]
        )
        grads.append(lax.psum_scatter(kernel, "seq", scatter_dimension=1, tiled=True))
        grad = grad + activation_slope(before.astype(jnp.float32), back_u)
    kernel_gradient = jnp.stack(grads[::-1])
    resident_blocks = rows // BLOCK
    block_partial_sums = (
        tracks.astype(jnp.float32).reshape(resident_blocks, BLOCK, tracks.shape[1]).sum(axis=1)
    )
    scale = jnp.sqrt(jnp.float32(EXONS * BLOCK))
    all_blocks = lax.all_gather(block_partial_sums, "seq", axis=0, tiled=True)
    labels = jnp.arange(all_blocks.shape[0], dtype=jnp.int32)
    counts = jnp.sum((exon_blocks[:, :, None] == labels[None, None, :]).astype(jnp.float32), axis=1)
    coverage = jnp.dot(counts, all_blocks, precision=lax.Precision.HIGHEST) / scale
    return (tracks, coverage, grad.astype(jnp.bfloat16), kernel_gradient)


def solution(mesh):
    return jax.shard_map(
        shards,
        mesh=mesh,
        in_specs=(
            P("seq", "chan"),
            P(None, None, None, "chan"),
            P(None, "chan"),
            P("seq", "chan"),
            P("seq", None),
        ),
        out_specs=(
            P("seq", "chan"),
            P("seq", "chan"),
            P("seq", "chan"),
            P(None, None, "seq", "chan"),
        ),
        check_vma=False,
    )
```

profile of v0, /device:TPU:2, one launch (start us, length us, event | category | flops | bytes accessed | tf_op | source)
XLA Modules:
  0.0 468.9 jit_solution(14514463337364591084)
XLA Ops:
  7.2 0.0 copy-start
  7.2 0.0 all-gather.9.cloned.1.call-start
  7.2 2.2 fusion.30
  9.4 0.0 all-gather.9.cloned.1.call-update
  9.4 0.0 all-gather.11.cloned.1.call-start
  9.5 1.3 collective-permute-start.1
  10.8 11.8 %collective-permute-done.1 = bf16[512,384]{1,0:T(8,128)(2,1)S(1)} collective-permute-done((bf16[512,384]{1,0:T(8,128)(2,1)}, bf16[512,384]{1,0:T(8,128)(2,1)S(1)}, u32[]{:S(2)}, u32[]{:S(2)}) %collective-permute-start.1) | collective-permute-done | bytes 393248 | tf_op jit(solution)/shard_map/ppermute | solution.py:13
  22.6 0.7 copy-done.8
  23.4 0.0 all-gather.11.cloned.1.call-update
  23.4 0.0 all-gather.7.cloned.1.call-start
  23.4 3.8 collective-permute-start
  27.3 8.0 %collective-permute-done = bf16[512,384]{1,0:T(8,128)(2,1)S(1)} collective-permute-done((bf16[512,384]{1,0:T(8,128)(2,1)}, bf16[512,384]{1,0:T(8,128)(2,1)S(1)}, u32[]{:S(2)}, u32[]{:S(2)}) %collective-permute-start) | collective-permute-done | bytes 393248 | tf_op jit(solution)/shard_map/ppermute | solution.py:13
  35.3 0.7 copy-done.9
  36.0 0.0 all-gather.7.cloned.1.call-update
  36.0 0.0 all-gather.13.cloned.1.call-start
  36.1 5.5 %all-gather.9.cloned.1.call-done = bf16[512,1536]{1,0:T(8,128)(2,1)} async-done(((bf16[512,384]{1,0:T(8,128)(2,1)}), bf16[512,1536]{1,0:T(8,128)(2,1)}) %all-gather.9.cloned.1.call-update) | async-done | bytes 1572880 | tf_op jit(solution)/shard_map/all_gather | solution.py:49
  41.5 3.6 fusion.10
  45.2 27.9 %all-gather.11.cloned.1.call-done = bf16[512,1536]{1,0:T(8,128)(2,1)} async-done(((bf16[512,384]{1,0:T(8,128)(2,1)}), bf16[512,1536]{1,0:T(8,128)(2,1)}) %all-gather.11.cloned.1.call-update) | async-done | bytes 1572880 | tf_op jit(solution)/shard_map/all_gather | solution.py:51
  73.1 3.6 fusion.6
  76.7 27.4 %all-gather.7.cloned.1.call-done = bf16[512,1536]{1,0:T(8,128)(2,1)} async-done(((bf16[512,384]{1,0:T(8,128)(2,1)}), bf16[512,1536]{1,0:T(8,128)(2,1)}) %all-gather.7.cloned.1.call-update) | async-done | bytes 1572880 | tf_op jit(solution)/shard_map/all_gather | solution.py:50
  104.1 0.0 copy-done.2
  104.1 3.9 fusion.3
  108.1 0.0 all-gather.13.cloned.1.call-update
  108.1 0.0 reduce-scatter.4.cloned.1.call-start
  108.1 29.2 %all-gather.13.cloned.1.call-done = bf16[512,1536]{1,0:T(8,128)(2,1)} async-done(((bf16[512,384]{1,0:T(8,128)(2,1)}), bf16[512,1536]{1,0:T(8,128)(2,1)}) %all-gather.13.cloned.1.call-update) | async-done | bytes 1572880 | tf_op jit(solution)/shard_map/all_gather | solution.py:59
  137.4 0.0 copy-done
  137.4 5.8 %convert_reduce_fusion = (f32[4,1024]{1,0:T(4,128)}, bf16[512,1024]{1,0:T(8,128)(2,1)}, f32[512,1024]{1,0:T(8,128)S(1)}) fusion(bf16[512,1536]{1,0:T(8,128)(2,1)} %all-gather.13.cloned.1.call-done, bf16[1536,1024]{1,0:T(8,128)(2,1)S(1)} %copy-done), kind=kOutput, calls=%fused_computation.8 | convolution fusion | flops 1615327232 | bytes 7880704 | tf_op jit(solution)/shard_map/dot_general | solution.py:60
  143.2 0.0 copy-done.12
  143.2 3.5 fusion.15
  146.7 0.0 reduce-scatter.4.cloned.1.call-update
  146.7 0.0 all-gather.15.cloned.1.call-start
  146.8 0.5 all-gather.15.cloned.1.call-update
  147.3 0.0 reduce-scatter.6.cloned.1.call-start
  147.3 40.1 %reduce-scatter.4.cloned.1.call-done = f32[512,384]{1,0:T(8,128)} async-done(((f32[512,1536]{1,0:T(8,128)}), f32[512,384]{1,0:T(8,128)}) %reduce-scatter.4.cloned.1.call-update) | async-done | bytes 786448 | tf_op jit(solution)/shard_map/reduce_scatter | solution.py:63
  187.4 1.2 convert_element_type.37
  188.6 0.0 copy-start.3
  188.6 0.0 copy-start.1
  188.6 3.7 collective-permute-start.3
  192.4 1.3 collective-permute-start.2
  193.7 2.3 fusion.8
  196.0 0.0 copy-done.3
  196.0 4.8 %collective-permute-done.3 = bf16[512,384]{1,0:T(8,128)(2,1)S(1)} collective-permute-done((bf16[512,384]{1,0:T(8,128)(2,1)S(1)}, bf16[512,384]{1,0:T(8,128)(2,1)S(1)}, u32[]{:S(2)}, u32[]{:S(2)}) %collective-permute-start.3) | collective-permute-done | bytes 393248 | tf_op jit(solution)/shard_map/ppermute | solution.py:13
  200.8 0.0 copy-done.1
  200.8 1.0 fusion.4
  201.8 3.1 collective-permute-done.2
  204.9 0.7 copy-done.4
  205.6 2.7 fusion
  208.4 0.0 reduce-scatter.6.cloned.1.call-update
  208.4 0.2 reduce-scatter.8.cloned.1.call-start
  208.6 0.0 copy-start.7
  208.6 2.6 convolution_bitcast_fusion.1
  211.3 0.0 copy-done.7
  211.3 1.0 convolution_bitcast_fusion
  212.3 1.0 convolution_bitcast_fusion.2
  213.3 3.3 pad_maximum_fusion
  216.7 0.0 reduce-scatter.8.cloned.1.call-update
  216.7 0.7 copy-done.10
  217.4 0.1 convert_reduce_fusion.1
  217.4 50.6 %all-gather.15.cloned.1.call-done = f32[64,4,1024]{2,1,0:T(4,128)} async-done(((f32[1,4,1024]{2,1,0:T(4,128)}), f32[64,4,1024]{2,1,0:T(4,128)}) %all-gather.15.cloned.1.call-update) | async-done | bytes 1048592 | tf_op jit(solution)/shard_map/all_gather | solution.py:87
  268.0 2.6 reshape.20
  270.6 2.4 convolution_multiply_fusion
  273.1 34.8 %reduce-scatter.6.cloned.1.call-done = f32[512,384]{1,0:T(8,128)} async-done(((f32[512,1536]{1,0:T(8,128)}), f32[512,384]{1,0:T(8,128)}) %reduce-scatter.6.cloned.1.call-update) | async-done | bytes 786448 | tf_op jit(solution)/shard_map/reduce_scatter | solution.py:75
  307.9 2.7 fusion.26
  310.6 151.5 %reduce-scatter.8.cloned.1.call-done = f32[3,24,384]{2,1,0:T(8,128)} async-done(((f32[3,1536,384]{2,1,0:T(8,128)}), f32[3,24,384]{2,1,0:T(8,128)}) %reduce-scatter.8.cloned.1.call-update) | async-done | bytes 110608 | tf_op jit(solution)/shard_map/reduce_scatter | solution.py:79
  (12 shorter events, 0.0 us)
Async XLA Ops:
  7.2 130.2 %copy-start = (bf16[1536,1024]{1,0:T(8,128)(2,1)S(1)}, bf16[1536,1024]{1,0:T(8,128)(2,1)}, u32[]{:S(2)}) copy-start(bf16[1536,1024]{1,0:T(8,128)(2,1)} %param.7) | copy-start | bytes 9437188
  7.2 34.4 %all-gather.9.cloned.1.call-start = ((), (), s32[]{:S(2)}) async-start(), calls=%async_computation.4 | async-start | bytes 1966080 | tf_op jit(solution)/shard_map/all_gather | solution.py:49
  9.4 63.7 %all-gather.11.cloned.1.call-start = ((), (), s32[]{:S(2)}) async-start(), calls=%async_computation.5 | async-start | bytes 1966080 | tf_op jit(solution)/shard_map/all_gather | solution.py:51
  9.5 13.1 %collective-permute-start.1 = (bf16[512,384]{1,0:T(8,128)(2,1)}, bf16[512,384]{1,0:T(8,128)(2,1)S(1)}, u32[]{:S(2)}, u32[]{:S(2)}) collective-permute-start(bf16[512,384]{1,0:T(8,128)(2,1)} %fusion.30), channel_id=1, source_target_pairs={{8,0},{12,4},{16,8},{20,12},{24,16},{28,20},{32,24},{36,28},{40,32... | collective-permute-start | bytes 1179656 | tf_op jit(solution)/shard_map/ppermute | solution.py:13
  22.6 0.7 copy-start.8
  23.4 80.7 %all-gather.7.cloned.1.call-start = ((), (), s32[]{:S(2)}) async-start(), calls=%async_computation.3 | async-start | bytes 1966080 | tf_op jit(solution)/shard_map/all_gather | solution.py:50
  23.4 11.8 %collective-permute-start = (bf16[512,384]{1,0:T(8,128)(2,1)}, bf16[512,384]{1,0:T(8,128)(2,1)S(1)}, u32[]{:S(2)}, u32[]{:S(2)}) collective-permute-start(bf16[512,384]{1,0:T(8,128)(2,1)} %fusion.30), channel_id=1, source_target_pairs={{0,8},{4,12},{8,16},{12,20},{16,24},{20,28},{24,32},{28,36},{32,40... | collective-permute-start | bytes 1179656 | tf_op jit(solution)/shard_map/ppermute | solution.py:13
  35.3 0.7 copy-start.9
  36.0 101.3 %all-gather.13.cloned.1.call-start = ((), (), s32[]{:S(2)}) async-start(), calls=%async_computation.6 | async-start | bytes 1966080 | tf_op jit(solution)/shard_map/all_gather | solution.py:59
  45.2 59.0 %copy-start.2 = (bf16[512,384]{1,0:T(8,128)(2,1)S(1)}, bf16[512,384]{1,0:T(8,128)(2,1)}, u32[]{:S(2)}) copy-start(bf16[512,384]{1,0:T(8,128)(2,1)} %param.5) | copy-start | bytes 1179652
  108.1 79.3 %reduce-scatter.4.cloned.1.call-start = ((), (), s32[]{:S(2)}) async-start(), calls=%async_computation.7 | async-start | bytes 3932160 | tf_op jit(solution)/shard_map/reduce_scatter | solution.py:63
  137.4 5.8 %copy-start.12 = (bf16[512,1024]{1,0:T(8,128)(2,1)S(1)}, bf16[512,1024]{1,0:T(8,128)(2,1)}, u32[]{:S(2)}) copy-start(bf16[512,1024]{1,0:T(8,128)(2,1)} %param.8) | copy-start | bytes 3145732
  146.7 121.3 %all-gather.15.cloned.1.call-start = ((), (), s32[]{:S(2)}) async-start(), calls=%async_computation.10 | async-start | bytes 1064960 | tf_op jit(solution)/shard_map/all_gather | solution.py:87
  147.3 160.6 %reduce-scatter.6.cloned.1.call-start = ((), (), s32[]{:S(2)}) async-start(), calls=%async_computation.8 | async-start | bytes 3932160 | tf_op jit(solution)/shard_map/reduce_scatter | solution.py:75
  188.6 7.4 %copy-start.3 = (bf16[512,384]{1,0:T(8,128)(2,1)}, bf16[512,384]{1,0:T(8,128)(2,1)S(1)}, u32[]{:S(2)}) copy-start(bf16[512,384]{1,0:T(8,128)(2,1)S(1)} %convert_element_type.37) | copy-start | bytes 1179652
  188.6 12.1 %copy-start.1 = (bf16[1,3,1536,384]{3,2,1,0:T(8,128)(2,1)S(1)}, bf16[1,3,1536,384]{3,2,1,0:T(8,128)(2,1)}, u32[]{:S(2)}) copy-start(bf16[1,3,1536,384]{3,2,1,0:T(8,128)(2,1)} %param.6) | copy-start | bytes 10616836
  188.6 12.1 %collective-permute-start.3 = (bf16[512,384]{1,0:T(8,128)(2,1)S(1)}, bf16[512,384]{1,0:T(8,128)(2,1)S(1)}, u32[]{:S(2)}, u32[]{:S(2)}) collective-permute-start(bf16[512,384]{1,0:T(8,128)(2,1)S(1)} %convert_element_type.37), channel_id=1, source_target_pairs={{0,8},{4,12},{8,16},{12,20},{16,24},{20,28},{24,32},{28,36},{32,40... | collective-permute-start | bytes 1179656 | tf_op jit(solution)/shard_map/ppermute | solution.py:13
  192.4 12.5 %collective-permute-start.2 = (bf16[512,384]{1,0:T(8,128)(2,1)S(1)}, bf16[512,384]{1,0:T(8,128)(2,1)S(1)}, u32[]{:S(2)}, u32[]{:S(2)}) collective-permute-start(bf16[512,384]{1,0:T(8,128)(2,1)S(1)} %convert_element_type.37), channel_id=1, source_target_pairs={{8,0},{12,4},{16,8},{20,12},{24,16},{28,20},{32,24},{36,28},{40,32... | collective-permute-start | bytes 1179656 | tf_op jit(solution)/shard_map/ppermute | solution.py:13
  200.8 1.0 copy-start.6
  204.9 0.7 copy-start.4
  208.4 253.7 %reduce-scatter.8.cloned.1.call-start = ((), (), s32[]{:S(2)}) async-start(), calls=%async_computation.9 | async-start | bytes 7188480 | tf_op jit(solution)/shard_map/reduce_scatter | solution.py:79
  208.6 2.7 copy-start.7
  208.6 2.6 copy-start.11
  211.3 1.0 copy-start.5
  216.7 0.7 copy-start.10
Sparse Core Ops, SparseCore 0:
  10.4 31.0 all-gather.8
  44.0 29.1 all-gather.10
  75.0 29.1 all-gather.6
  108.2 29.1 all-gather.12
  146.8 40.5 reduce-scatter.3
  190.6 77.3 all-gather.14
  270.6 37.2 reduce-scatter.5
  312.7 149.2 reduce-scatter.7
where the time goes:
time: 469 us
  waiting for transfers between devices  395 us (84%)
  matrix products  33.6 us (7%)
  between operations  14.3 us (3%)
  starting transfers between devices  10.7 us (2%)
  other arithmetic  9.47 us (2%)
  local copies, waits for them, and re-layouts  5.52 us (1%)
    reduce_scatter x1, waiting for transfers between devices, shards(): lax.psum_scatter(kernel, 'seq', scatter_dimension=1, tiled=True)  151 us
    all_gather x1, waiting for transfers between devices, shards(): all_blocks = lax.all_gather(block_partial_sums, 'seq', axis=0, tiled=True)  50.6 us
    reduce_scatter x1, waiting for transfers between devices, shards(): lax.psum_scatter(times_t(head_term, head_weight), 'chan', scatter_dimensi...  40.1 us
    reduce_scatter x1, waiting for transfers between devices, shards(): lax.psum_scatter(partial_value, 'chan', scatter_dimension=1, tiled=True)  34.8 us
    all_gather x1, waiting for transfers between devices, shards(): full_state = lax.all_gather(state, 'chan', axis=1, tiled=True)  29.2 us
    all_gather x1, waiting for transfers between devices, shards(): whole_up = lax.all_gather(upper, 'chan', axis=1, tiled=True)  27.9 us
    ppermute x4, waiting for transfers between devices, shifted(): lax.ppermute(value, axis, [(source, source + steps) for source in range(l...  27.7 us
    all_gather x1, waiting for transfers between devices, shards(): whole_low = lax.all_gather(lower, 'chan', axis=1, tiled=True)  27.4 us
  transfers between devices with their start and end apart: 12, of which 12 were waited for; matrix products, arithmetic and copies ran while one was open for 6% of the time, Pallas kernels for 0%

commit v1 on v0

--- a/solution.py
+++ b/solution.py
@@ -48,7 +48,12 @@
     upper = tap_input(acted, -steps)
     whole = lax.all_gather(acted, "chan", axis=1, tiled=True)
     whole_low = lax.all_gather(lower, "chan", axis=1, tiled=True)
-    whole_up = lax.all_gather(upper, "chan", axis=1, tiled=True)
+    ring = [upper]
+    for hop in range(3):
+        ring.append(lax.ppermute(ring[-1], "chan", [(dev, (dev + 1) % 4) for dev in range(4)]))
+    whole_up = jnp.roll(
+        jnp.concatenate(ring[::-1], axis=1), (lax.axis_index("chan") + 1) * ring[0].shape[1], axis=1
+    )
     mixed = jnp.dot(whole_low, conv_weight[layer_number, 0], preferred_element_type=jnp.float32)
     mixed = mixed + jnp.dot(whole, conv_weight[layer_number, 1], preferred_element_type=jnp.float32)
     mixed = mixed + jnp.dot(

time: 469 us -> 447 us (0.953)
  waiting for transfers between devices: 395 us -> 362 us
  local copies, waits for them, and re-layouts: 5.52 us -> 11.5 us
  starting transfers between devices: 10.7 us -> 16.2 us
    ppermute x0 -> x3, waiting for transfers between devices: none -> 36.2 us  [shards(): lax.ppermute(ring[-1], 'chan', [(dev, (dev + 1) % 4) for dev in range(4)])]
    all_gather x1 -> x0, waiting for transfers between devices: 27.9 us -> none  [shards(): whole_up = lax.all_gather(upper, 'chan', axis=1, tiled=True)]
    all_gather x1, waiting for transfers between devices: 27.4 us -> 5.08 us  [shards(): whole_low = lax.all_gather(lower, 'chan', axis=1, tiled=True)]
    ppermute x4, waiting for transfers between devices: 27.7 us -> 13.5 us  [shifted(): lax.ppermute(value, axis, [(source, source + steps) for source in range(l...]
    unnamed x27 -> x30, local copies, waits for them, and re-layouts: 5.52 us -> 11.4 us
    all_gather x1, waiting for transfers between devices: 5.46 us -> 0.01 us  [shards(): whole = lax.all_gather(acted, 'chan', axis=1, tiled=True)]
  transfers between devices with their start and end apart: 12 -> 14, of which waited for: 12 -> 12; matrix products, arithmetic and copies ran while one was open for 6% -> 8% of each run, Pallas kernels for 0% -> 0%
where the time goes in v1:
time: 447 us
  waiting for transfers between devices  362 us (81%)
  matrix products  33.2 us (7%)
  starting transfers between devices  16.2 us (4%)
  between operations  14.3 us (3%)
  local copies, waits for them, and re-layouts  11.5 us (3%)
  other arithmetic  9.61 us (2%)
    reduce_scatter x1, waiting for transfers between devices, shards(): lax.psum_scatter(kernel, 'seq', scatter_dimension=1, tiled=True)  151 us
    all_gather x1, waiting for transfers between devices, shards(): all_blocks = lax.all_gather(block_partial_sums, 'seq', axis=0, tiled=True)  50.9 us
    reduce_scatter x1, waiting for transfers between devices, shards(): lax.psum_scatter(times_t(head_term, head_weight), 'chan', scatter_dimensi...  40.1 us
    ppermute x3, waiting for transfers between devices, shards(): lax.ppermute(ring[-1], 'chan', [(dev, (dev + 1) % 4) for dev in range(4)])  36.2 us
    reduce_scatter x1, waiting for transfers between devices, shards(): lax.psum_scatter(partial_value, 'chan', scatter_dimension=1, tiled=True)  34.6 us
    all_gather x1, waiting for transfers between devices, shards(): full_state = lax.all_gather(state, 'chan', axis=1, tiled=True)  29.2 us
    ppermute x4, waiting for transfers between devices, shifted(): lax.ppermute(value, axis, [(source, source + steps) for source in range(l...  13.5 us
    ppermute x4, starting transfers between devices, shifted(): lax.ppermute(value, axis, [(source, source + steps) for source in range(l...  11.6 us
  transfers between devices with their start and end apart: 14, of which 12 were waited for; matrix products, arithmetic and copies ran while one was open for 8% of the time, Pallas kernels for 0%

profile of v1, /device:TPU:2, one launch (start us, length us, event | category | flops | bytes accessed | tf_op | source)
XLA Modules:
  0.0 446.5 jit_solution(15942412659161946553)
XLA Ops:
  7.2 0.0 copy-start
  7.2 0.0 all-gather.8.cloned.1.call-start
  7.2 2.2 fusion.31
  9.4 0.0 all-gather.8.cloned.1.call-update
  9.4 0.0 all-gather.6.cloned.1.call-start
  9.5 1.3 collective-permute-start.1
  10.8 5.3 %collective-permute-start = (bf16[512,384]{1,0:T(8,128)(2,1)}, bf16[512,384]{1,0:T(8,128)(2,1)}, u32[]{:S(2)}, u32[]{:S(2)}) collective-permute-start(bf16[512,384]{1,0:T(8,128)(2,1)} %fusion.31), channel_id=1, source_target_pairs={{0,8},{4,12},{8,16},{12,20},{16,24},{20,28},{24,32},{28,36},{32,40... | collective-permute-start | bytes 1179656 | tf_op jit(solution)/shard_map/ppermute | solution.py:13
  16.1 6.5 %collective-permute-done.1 = bf16[512,384]{1,0:T(8,128)(2,1)S(1)} collective-permute-done((bf16[512,384]{1,0:T(8,128)(2,1)}, bf16[512,384]{1,0:T(8,128)(2,1)S(1)}, u32[]{:S(2)}, u32[]{:S(2)}) %collective-permute-start.1) | collective-permute-done | bytes 393248 | tf_op jit(solution)/shard_map/ppermute | solution.py:13
  22.6 1.5 collective-permute-start.2
  24.1 0.0 all-gather.6.cloned.1.call-update
  24.1 0.0 all-gather.10.cloned.1.call-start
  24.2 17.1 %collective-permute-done.2 = bf16[512,384]{1,0:T(8,128)(2,1)} collective-permute-done((bf16[512,384]{1,0:T(8,128)(2,1)S(1)}, bf16[512,384]{1,0:T(8,128)(2,1)}, u32[]{:S(2)}, u32[]{:S(2)}) %collective-permute-start.2) | collective-permute-done | bytes 393248 | tf_op jit(solution)/shard_map/ppermute | solution.py:53
  41.2 1.4 collective-permute-start.3
  42.6 11.3 %collective-permute-done.3 = bf16[512,384]{1,0:T(8,128)(2,1)} collective-permute-done((bf16[512,384]{1,0:T(8,128)(2,1)}, bf16[512,384]{1,0:T(8,128)(2,1)}, u32[]{:S(2)}, u32[]{:S(2)}) %collective-permute-start.3) | collective-permute-done | bytes 393248 | tf_op jit(solution)/shard_map/ppermute | solution.py:53
  54.0 1.5 collective-permute-start.4
  55.5 7.8 %collective-permute-done.4 = bf16[512,384]{1,0:T(8,128)(2,1)} collective-permute-done((bf16[512,384]{1,0:T(8,128)(2,1)}, bf16[512,384]{1,0:T(8,128)(2,1)}, u32[]{:S(2)}, u32[]{:S(2)}) %collective-permute-start.4) | collective-permute-done | bytes 393248 | tf_op jit(solution)/shard_map/ppermute | solution.py:53
  63.3 1.1 constant_dynamic-update-slice_fusion.7
  64.3 1.1 constant_dynamic-update-slice_fusion.6
  65.4 1.1 constant_dynamic-update-slice_fusion.5
  66.6 0.1 constant_dynamic-update-slice_fusion.4
  66.7 1.1 constant_dynamic-update-slice_fusion.3
  67.8 1.1 constant_dynamic-update-slice_fusion.2
  68.9 1.1 constant_dynamic-update-slice_fusion.1
  70.0 0.1 constant_dynamic-update-slice_fusion
  70.1 3.2 fusion.2
  73.3 3.7 fusion.11
  77.0 5.1 %all-gather.6.cloned.1.call-done = bf16[512,1536]{1,0:T(8,128)(2,1)} async-done(((bf16[512,384]{1,0:T(8,128)(2,1)}), bf16[512,1536]{1,0:T(8,128)(2,1)}) %all-gather.6.cloned.1.call-update) | async-done | bytes 1572880 | tf_op jit(solution)/shard_map/all_gather | solution.py:50
  82.1 3.9 fusion.5
  86.0 0.0 all-gather.10.cloned.1.call-update
  86.0 0.0 reduce-scatter.4.cloned.1.call-start
  86.1 29.2 %all-gather.10.cloned.1.call-done = bf16[512,1536]{1,0:T(8,128)(2,1)} async-done(((bf16[512,384]{1,0:T(8,128)(2,1)}), bf16[512,1536]{1,0:T(8,128)(2,1)}) %all-gather.10.cloned.1.call-update) | async-done | bytes 1572880 | tf_op jit(solution)/shard_map/all_gather | solution.py:64
  115.3 5.8 %convert_reduce_fusion = (f32[4,1024]{1,0:T(4,128)}, bf16[512,1024]{1,0:T(8,128)(2,1)}, f32[512,1024]{1,0:T(8,128)S(1)}) fusion(bf16[512,1536]{1,0:T(8,128)(2,1)} %all-gather.10.cloned.1.call-done, bf16[1536,1024]{1,0:T(8,128)(2,1)S(1)} %copy-done), kind=kOutput, calls=%fused_computation.8 | convolution fusion | flops 1615327232 | bytes 7880704 | tf_op jit(solution)/shard_map/dot_general | solution.py:65
  121.2 3.5 fusion.16
  124.6 0.0 reduce-scatter.4.cloned.1.call-update
  124.6 0.0 all-gather.12.cloned.1.call-start
  124.7 0.5 all-gather.12.cloned.1.call-update
  125.2 0.0 reduce-scatter.6.cloned.1.call-start
  125.3 40.1 %reduce-scatter.4.cloned.1.call-done = f32[512,384]{1,0:T(8,128)} async-done(((f32[512,1536]{1,0:T(8,128)}), f32[512,384]{1,0:T(8,128)}) %reduce-scatter.4.cloned.1.call-update) | async-done | bytes 786448 | tf_op jit(solution)/shard_map/reduce_scatter | solution.py:68
  165.3 1.3 convert_element_type.37
  166.7 3.5 collective-permute-start.6
  170.2 1.5 collective-permute-start.5
  171.7 2.3 fusion.9
  173.9 4.6 %collective-permute-done.6 = bf16[512,384]{1,0:T(8,128)(2,1)S(1)} collective-permute-done((bf16[512,384]{1,0:T(8,128)(2,1)S(1)}, bf16[512,384]{1,0:T(8,128)(2,1)S(1)}, u32[]{:S(2)}, u32[]{:S(2)}) %collective-permute-start.6) | collective-permute-done | bytes 393248 | tf_op jit(solution)/shard_map/ppermute | solution.py:13
  178.6 0.7 copy-done.6
  179.3 1.0 fusion.6
  180.3 2.4 collective-permute-done.5
  182.7 0.7 copy-done.4
  183.4 2.7 fusion
  186.2 0.0 reduce-scatter.6.cloned.1.call-update
  186.2 0.0 reduce-scatter.8.cloned.1.call-start
  186.2 0.0 copy-start.7
  186.3 2.6 convolution_bitcast_fusion.1
  188.9 1.0 convolution_bitcast_fusion
  189.9 1.0 convolution_bitcast_fusion.2
  190.9 3.3 pad_maximum_fusion
  194.3 0.0 reduce-scatter.8.cloned.1.call-update
  194.3 0.7 copy-done.8
  195.0 0.1 convert_reduce_fusion.1
  195.1 50.9 %all-gather.12.cloned.1.call-done = f32[64,4,1024]{2,1,0:T(4,128)} async-done(((f32[1,4,1024]{2,1,0:T(4,128)}), f32[64,4,1024]{2,1,0:T(4,128)}) %all-gather.12.cloned.1.call-update) | async-done | bytes 1048592 | tf_op jit(solution)/shard_map/all_gather | solution.py:92
  246.0 2.6 reshape.20
  248.5 2.4 convolution_multiply_fusion
  251.0 34.6 %reduce-scatter.6.cloned.1.call-done = f32[512,384]{1,0:T(8,128)} async-done(((f32[512,1536]{1,0:T(8,128)}), f32[512,384]{1,0:T(8,128)}) %reduce-scatter.6.cloned.1.call-update) | async-done | bytes 786448 | tf_op jit(solution)/shard_map/reduce_scatter | solution.py:80
  285.6 2.7 fusion.27
  288.3 151.3 %reduce-scatter.8.cloned.1.call-done = f32[3,24,384]{2,1,0:T(8,128)} async-done(((f32[3,1536,384]{2,1,0:T(8,128)}), f32[3,24,384]{2,1,0:T(8,128)}) %reduce-scatter.8.cloned.1.call-update) | async-done | bytes 110608 | tf_op jit(solution)/shard_map/reduce_scatter | solution.py:84
  (19 shorter events, 0.0 us)
Async XLA Ops:
  7.2 108.1 %copy-start = (bf16[1536,1024]{1,0:T(8,128)(2,1)S(1)}, bf16[1536,1024]{1,0:T(8,128)(2,1)}, u32[]{:S(2)}) copy-start(bf16[1536,1024]{1,0:T(8,128)(2,1)} %param.7) | copy-start | bytes 9437188
  7.2 66.1 %all-gather.8.cloned.1.call-start = ((), (), s32[]{:S(2)}) async-start(), calls=%async_computation.4 | async-start | bytes 1966080 | tf_op jit(solution)/shard_map/all_gather | solution.py:49
  9.4 72.6 %all-gather.6.cloned.1.call-start = ((), (), s32[]{:S(2)}) async-start(), calls=%async_computation.3 | async-start | bytes 1966080 | tf_op jit(solution)/shard_map/all_gather | solution.py:50
  9.5 13.1 %collective-permute-start.1 = (bf16[512,384]{1,0:T(8,128)(2,1)}, bf16[512,384]{1,0:T(8,128)(2,1)S(1)}, u32[]{:S(2)}, u32[]{:S(2)}) collective-permute-start(bf16[512,384]{1,0:T(8,128)(2,1)} %fusion.31), channel_id=1, source_target_pairs={{8,0},{12,4},{16,8},{20,12},{24,16},{28,20},{32,24},{36,28},{40,32... | collective-permute-start | bytes 1179656 | tf_op jit(solution)/shard_map/ppermute | solution.py:13
  10.8 13.3 %collective-permute-start = (bf16[512,384]{1,0:T(8,128)(2,1)}, bf16[512,384]{1,0:T(8,128)(2,1)}, u32[]{:S(2)}, u32[]{:S(2)}) collective-permute-start(bf16[512,384]{1,0:T(8,128)(2,1)} %fusion.31), channel_id=1, source_target_pairs={{0,8},{4,12},{8,16},{12,20},{16,24},{20,28},{24,32},{28,36},{32,40... | collective-permute-start | bytes 1179656 | tf_op jit(solution)/shard_map/ppermute | solution.py:13
  22.6 18.6 %collective-permute-start.2 = (bf16[512,384]{1,0:T(8,128)(2,1)S(1)}, bf16[512,384]{1,0:T(8,128)(2,1)}, u32[]{:S(2)}, u32[]{:S(2)}) collective-permute-start(bf16[512,384]{1,0:T(8,128)(2,1)S(1)} %collective-permute-done.1), channel_id=1, source_target_pairs={{0,1},{1,2},{2,3},{3,0},{4,5},{5,6},{6,7},{7,4},{8,9},{9,10},{10,1... | collective-permute-start | bytes 1179656 | tf_op jit(solution)/shard_map/ppermute | solution.py:53
  24.1 91.2 %all-gather.10.cloned.1.call-start = ((), (), s32[]{:S(2)}) async-start(), calls=%async_computation.5 | async-start | bytes 1966080 | tf_op jit(solution)/shard_map/all_gather | solution.py:64
  41.2 12.7 %collective-permute-start.3 = (bf16[512,384]{1,0:T(8,128)(2,1)}, bf16[512,384]{1,0:T(8,128)(2,1)}, u32[]{:S(2)}, u32[]{:S(2)}) collective-permute-start(bf16[512,384]{1,0:T(8,128)(2,1)} %collective-permute-done.2), channel_id=1, source_target_pairs={{0,1},{1,2},{2,3},{3,0},{4,5},{5,6},{6,7},{7,4},{8,9},{9,10},{10,1... | collective-permute-start | bytes 1179656 | tf_op jit(solution)/shard_map/ppermute | solution.py:53
  54.0 9.3 %collective-permute-start.4 = (bf16[512,384]{1,0:T(8,128)(2,1)}, bf16[512,384]{1,0:T(8,128)(2,1)}, u32[]{:S(2)}, u32[]{:S(2)}) collective-permute-start(bf16[512,384]{1,0:T(8,128)(2,1)} %collective-permute-done.3), channel_id=1, source_target_pairs={{0,1},{1,2},{2,3},{3,0},{4,5},{5,6},{6,7},{7,4},{8,9},{9,10},{10,1... | collective-permute-start | bytes 1179656 | tf_op jit(solution)/shard_map/ppermute | solution.py:53
  73.3 8.8 %copy-start.2 = (bf16[512,384]{1,0:T(8,128)(2,1)S(1)}, bf16[512,384]{1,0:T(8,128)(2,1)}, u32[]{:S(2)}) copy-start(bf16[512,384]{1,0:T(8,128)(2,1)} %param.5) | copy-start | bytes 1179652
  86.0 79.3 %reduce-scatter.4.cloned.1.call-start = ((), (), s32[]{:S(2)}) async-start(), calls=%async_computation.6 | async-start | bytes 3932160 | tf_op jit(solution)/shard_map/reduce_scatter | solution.py:68
  115.3 5.8 %copy-start.10 = (bf16[512,1024]{1,0:T(8,128)(2,1)S(1)}, bf16[512,1024]{1,0:T(8,128)(2,1)}, u32[]{:S(2)}) copy-start(bf16[512,1024]{1,0:T(8,128)(2,1)} %param.8) | copy-start | bytes 3145732
  124.6 121.3 %all-gather.12.cloned.1.call-start = ((), (), s32[]{:S(2)}) async-start(), calls=%async_computation.9 | async-start | bytes 1064960 | tf_op jit(solution)/shard_map/all_gather | solution.py:92
  125.2 160.4 %reduce-scatter.6.cloned.1.call-start = ((), (), s32[]{:S(2)}) async-start(), calls=%async_computation.7 | async-start | bytes 3932160 | tf_op jit(solution)/shard_map/reduce_scatter | solution.py:80
  165.3 14.0 %copy-start.1 = (bf16[1,3,1536,384]{3,2,1,0:T(8,128)(2,1)S(1)}, bf16[1,3,1536,384]{3,2,1,0:T(8,128)(2,1)}, u32[]{:S(2)}) copy-start(bf16[1,3,1536,384]{3,2,1,0:T(8,128)(2,1)} %param.6) | copy-start | bytes 10616836
  166.7 13.7 %copy-start.3 = (bf16[512,384]{1,0:T(8,128)(2,1)}, bf16[512,384]{1,0:T(8,128)(2,1)S(1)}, u32[]{:S(2)}) copy-start(bf16[512,384]{1,0:T(8,128)(2,1)S(1)} %convert_element_type.37) | copy-start | bytes 1179652
  166.7 11.9 %collective-permute-start.6 = (bf16[512,384]{1,0:T(8,128)(2,1)S(1)}, bf16[512,384]{1,0:T(8,128)(2,1)S(1)}, u32[]{:S(2)}, u32[]{:S(2)}) collective-permute-start(bf16[512,384]{1,0:T(8,128)(2,1)S(1)} %convert_element_type.37), channel_id=1, source_target_pairs={{0,8},{4,12},{8,16},{12,20},{16,24},{20,28},{24,32},{28,36},{32,40... | collective-permute-start | bytes 1179656 | tf_op jit(solution)/shard_map/ppermute | solution.py:13
  170.2 12.5 %collective-permute-start.5 = (bf16[512,384]{1,0:T(8,128)(2,1)S(1)}, bf16[512,384]{1,0:T(8,128)(2,1)S(1)}, u32[]{:S(2)}, u32[]{:S(2)}) collective-permute-start(bf16[512,384]{1,0:T(8,128)(2,1)S(1)} %convert_element_type.37), channel_id=1, source_target_pairs={{8,0},{12,4},{16,8},{20,12},{24,16},{28,20},{32,24},{36,28},{40,32... | collective-permute-start | bytes 1179656 | tf_op jit(solution)/shard_map/ppermute | solution.py:13
  178.6 0.7 copy-start.6
  182.7 0.7 copy-start.4
  186.2 253.5 %reduce-scatter.8.cloned.1.call-start = ((), (), s32[]{:S(2)}) async-start(), calls=%async_computation.8 | async-start | bytes 7188480 | tf_op jit(solution)/shard_map/reduce_scatter | solution.py:84
  186.2 2.6 copy-start.7
  186.3 2.6 copy-start.9
  188.9 1.0 copy-start.5
  194.3 0.7 copy-start.8
Sparse Core Ops, SparseCore 0:
  10.4 40.3 all-gather.7
  52.6 29.3 all-gather.5
  86.1 29.1 all-gather.9
  124.8 40.5 reduce-scatter.3
  168.5 77.3 all-gather.11
  248.4 37.2 reduce-scatter.5
  290.5 149.1 reduce-scatter.7
